TPU v7x, 256 devices: a whole 4x4x8 slice. The times are simulated.
256 devices in a mesh: track: 16 (over y, z_hi), rep: 16 (over x, z_lo, core).
Axes of the slice: x: 4, y: 4, z: 8 (z_hi: 4, z_lo: 2; z = z_hi * 2 + z_lo), core: 2. Of those that a mesh axis runs over, the one named last changes fastest.
Arguments:
- features: bfloat16 [16, 32, 32, 2048], P('rep', None, None, 'track'), may hold values from -6 to 6
- kernel_one: bfloat16 [5, 5, 32, 128], replicated, may hold values from -0.21875 to 0.21875
- kernel_two: bfloat16 [3, 3, 128, 128], replicated, may hold values from -0.1875 to 0.1875
- cotangent: bfloat16 [16, 128, 32, 2048], P('rep', None, None, 'track'), may hold values from -0.005859375 to 0.005859375
Outputs:
- feature_map: bfloat16 [16, 128, 32, 2048], P('rep', None, None, 'track')
- grad_one: float32 [5, 5, 32, 128], replicated
- grad_two: float32 [3, 3, 128, 128], replicated
All inputs are finite; a program needn't handle non-finite values.
Results may differ from a plain program's by a relative error of at most 0.006.
Values may be sent and summed in bfloat16 or wider, within the bound.
No kernel may reach another device: no remote copies, remote signals or barrier semaphores. Data moves between devices by JAX's collectives and lax.ppermute only.
A program may use at most 64 MiB of HBM per device.

v0:
```python
import jax
import jax.numpy as jnp
from jax import lax
from jax.sharding import PartitionSpec as P

scale_a = 0.7978845608
scale_b = 0.044715


def extended(block, sides, width):
    for axis, dim in sides:
        count = lax.axis_size(axis)
        forward = [(i, i + 1) for i in range(count - 1)]
        backward = [(target, source) for source, target in forward]
        low = lax.ppermute(
            lax.slice_in_dim(block, block.shape[dim] - width, None, axis=dim), axis, forward
        )
        high = lax.ppermute(lax.slice_in_dim(block, 0, width, axis=dim), axis, backward)
        block = jnp.concatenate([low, block, high], axis=dim)
    return block


def gelu(values):
    tangent = jnp.tanh(scale_a * (values + scale_b * values * values * values))
    return 0.5 * values * (1.0 + tangent)


def gelu_slope(values):
    tangent = jnp.tanh(scale_a * (values + scale_b * values * values * values))
    return 0.5 * (1.0 + tangent) + 0.5 * values * (1.0 - tangent * tangent) * scale_a * (
        1.0 + 3.0 * scale_b * values * values
    )


def convolve(lhs, kernel, dilation):
    return lax.conv_general_dilated(
        lhs,
        kernel,
        (1, 1),
        ((2, 2), (0, 0)),
        rhs_dilation=(dilation, dilation),
        dimension_numbers=("NCHW", "HWIO", "NCHW"),
        preferred_element_type=jnp.float32,
    )


def pad_rows(array):
    return jnp.pad(array, ((0, 0), (0, 0), (2, 2), (0, 0)))


def kernel_grad(padded, delta, taps, dilation):
    row_count = delta.shape[2]
    col_count = delta.shape[3]
    row_list = []
    for row_tap in range(taps):
        col_list = []
        for col_tap in range(taps):
            window = padded[
                :,
                :,
                dilation * row_tap : dilation * row_tap + row_count,
                dilation * col_tap : dilation * col_tap + col_count,
            ]
            col_list.append(
                jnp.einsum("nchw,nfhw->cf", window, delta, preferred_element_type=jnp.float32)
            )
        row_list.append(jnp.stack(col_list))
    return jnp.stack(row_list)


def on_device(features, kernel_one, kernel_two, cotangent):
    x_cols = extended(features, (("track", 3),), 2)
    pre_one = convolve(x_cols, kernel_one, 1)
    hidden = gelu(pre_one).astype(jnp.bfloat16)
    h_cols = extended(hidden, (("track", 3),), 2)
    pre_two = convolve(h_cols, kernel_two, 2)
    feature_map = gelu(pre_two).astype(jnp.bfloat16)
    delta_two = (cotangent.astype(jnp.float32) * gelu_slope(pre_two)).astype(jnp.bfloat16)
    local_two = kernel_grad(pad_rows(h_cols), delta_two, 3, 2)
    d_cols = extended(delta_two, (("track", 3),), 2)
    flipped = jnp.transpose(kernel_two[::-1, ::-1], (0, 1, 3, 2))
    back_hidden = convolve(d_cols, flipped, 2)
    delta_one = (back_hidden * gelu_slope(pre_one)).astype(jnp.bfloat16)
    local_one = kernel_grad(pad_rows(x_cols), delta_one, 5, 1)
    grad_one, grad_two = lax.psum((local_one, local_two), ("track", "rep"))
    return (feature_map, grad_one, grad_two)


def solution(mesh):
    placed = (P("rep", None, None, "track"), P(), P(), P("rep", None, None, "track"))
    return jax.shard_map(
        on_device,
        mesh=mesh,
        in_specs=placed,
        out_specs=(P("rep", None, None, "track"), P(), P()),
        check_vma=False,
    )
```

profile of v0, /device:TPU:2, one launch (start us, length us, event | category | flops | bytes accessed | tf_op | source)
XLA Modules:
  0.0 390.3 jit_solution(2140565538895657970)
XLA Ops:
  7.2 1.9 constant_dynamic-update-slice_fusion.1
  9.3 1.3 collective-permute-start.1
  10.6 5.8 %collective-permute-start = (bf16[1,32,32,2]{3,1,2,0:T(8,128)(2,1)S(1)}, bf16[1,32,32,2]{3,1,2,0:T(8,128)(2,1)S(1)}, u32[]{:S(2)}, u32[]{:S(2)}) collective-permute-start(bf16[1,32,32,2]{3,1,2,0:T(8,128)(2,1)S(1)} %get-tuple-element.19), channel_id=1, source_target_pairs={{0,16},{16,32},{32,48},{48,64},{64,80},{80,96},{96,112},{112,128},... | collective-permute-start | bytes 12296 | tf_op jit(solution)/shard_map/ppermute | solution.py:15
  16.4 2.3 copy.69
  18.7 7.6 %collective-permute-done.1 = bf16[1,32,32,2]{3,1,2,0:T(8,128)(2,1)S(1)} collective-permute-done((bf16[1,32,32,2]{3,1,2,0:T(8,128)(2,1)S(1)}, bf16[1,32,32,2]{3,1,2,0:T(8,128)(2,1)S(1)}, u32[]{:S(2)}, u32[]{:S(2)}) %collective-permute-start.1) | collective-permute-done | bytes 4128 | tf_op jit(solution)/shard_map/ppermute | solution.py:18
  27.1 1.4 copy.92
  28.7 1.7 copy.58
  30.4 1.0 slice.177
  31.5 6.9 %multiply_convert_fusion.1 = (bf16[32,8,17,128]{3,1,2,0:T(8,128)(2,1)S(1)}, f32[32,8,17,128]{3,1,2,0:T(8,128)}) fusion(pred[8,17]{0,1:T(8,128)(4,1)S(1)} %copy-done.15, bf16[5,5,32,128]{3,2,1,0:T(8,128)(2,1)S(1)} %copy-done.14, bf16[32,32,1,7,4]{0,3,4,1,2:T(8,128)(2,1)S(1)} %slice.177, bf16[32,32,1,8,17]{0,3,4,1,2:T(8,128)(2,1)} %copy.58), kind=kOutput, calls=%fused_computation.22 | convolution fusion | flops 864468992 | bytes 3883144 | tf_op jit(solution)/shard_map/conv_general_dilated | solution.py:36
  38.6 1.0 copy.90
  39.6 1.4 fusion.196
  41.0 1.6 copy.62
  42.6 1.3 collective-permute-start.3
  44.3 7.8 %collective-permute-start.2 = (bf16[1,128,32,2]{1,2,3,0:T(8,128)(2,1)S(1)}, bf16[1,128,32,2]{1,2,3,0:T(8,128)(2,1)S(1)}, u32[]{:S(2)}, u32[]{:S(2)}) collective-permute-start(bf16[1,128,32,2]{1,2,3,0:T(8,128)(2,1)S(1)} %copy.61), channel_id=1, source_target_pairs={{0,16},{16,32},{32,48},{48,64},{64,80},{80,96},{96,112},{112,128},... | collective-permute-start | bytes 49160 | tf_op jit(solution)/shard_map/ppermute | solution.py:15
  52.1 1.7 constant_dynamic-update-slice_fusion
  54.4 1.4 copy.63
  55.8 3.9 fusion.230
  59.7 2.5 pad_maximum_fusion
  62.2 3.0 copy.93
  65.9 5.0 %fusion.12 = (f32[32,8,17,128]{3,1,2,0:T(8,128)S(1)}, bf16[32,8,17,128]{3,1,2,0:T(8,128)(2,1)}) fusion(pred[8,17]{0,1:T(8,128)(4,1)S(1)} %copy-done.15, bf16[3,3,128,128]{3,2,1,0:T(8,128)(2,1)S(1)} %copy-done, bf16[128,32,1,7,4]{0,3,4,1,2:T(8,128)(2,1)S(1)} %slice.181, bf16[128,32,1,8,17]{0,3,4,1,2:T(8,128)(2,1)S(1)} %copy.67), kind=kOutput, calls=%fused_computation.18 | convolution fusion | flops 1245249536 | bytes 4980872 | tf_op jit(solution)/shard_map/conv_general_dilated | solution.py:36
  73.5 1.9 copy.78
  75.5 2.3 convolution_bitcast_fusion
  83.1 1.3 collective-permute-start.5
  84.4 7.4 %collective-permute-start.4 = (bf16[1,128,32,2]{1,2,3,0:T(8,128)(2,1)S(1)}, bf16[1,128,32,2]{1,2,3,0:T(8,128)(2,1)S(1)}, u32[]{:S(2)}, u32[]{:S(2)}) collective-permute-start(bf16[1,128,32,2]{1,2,3,0:T(8,128)(2,1)S(1)} %get-tuple-element.13), channel_id=1, source_target_pairs={{0,16},{16,32},{32,48},{48,64},{64,80},{80,96},{96,112},{112,128},... | collective-permute-start | bytes 49160 | tf_op jit(solution)/shard_map/ppermute | solution.py:15
  91.8 0.9 pad_maximum_fusion.3
  93.8 0.9 copy-done.17
  94.7 3.9 %fusion.7 = bf16[32,8,17,128]{3,1,2,0:T(8,128)(2,1)S(1)} fusion(f32[32,8,17,128]{3,1,2,0:T(8,128)S(1)} %copy-done.17, bf16[3,3,128,128]{3,2,1,0:T(8,128)(2,1)S(1)} %copy-done, bf16[128,32,1,7,4]{0,3,4,1,2:T(8,128)(2,1)S(1)} %slice.186, bf16[128,32,1,8,17]{0,3,4,1,2:T(8,128)(2,1)S(1)} %copy.72, pred[8,17]{0,1:T(8,128)(4,1)S(1)} %copy-done.16), kind=kOutput, calls=%fused_computation.13 | convolution fusion | flops 1245806592 | bytes 4980872 | tf_op jit(solution)/shard_map/conv_general_dilated | solution.py:36
  98.9 1.0 copy.91
  115.6 2.3 copy.89
  117.8 262.0 %all-reduce.5.cloned.1.call-done = (f32[5,5,32,128]{3,2,1,0:T(8,128)}, f32[3,3,128,128]{3,2,1,0:T(8,128)}) async-done(((f32[5,5,32,128]{3,2,1,0:T(8,128)}, f32[3,3,128,128]{3,2,1,0:T(8,128)}), (f32[5,5,32,128]{3,2,1,0:T(8,128)}, f32[3,3,128,128]{3,2,1,0:T(8,128)})) %all-reduce.5.cloned.1.call-update) | async-done | bytes 999440 | tf_op jit(solution)/shard_map/psum | solution.py:85
  379.8 1.8 copy.125
  381.5 1.9 copy.126
  (103 shorter events, 27.6 us)
Async XLA Ops:
  7.2 58.7 %copy-start = (bf16[3,3,128,128]{3,2,1,0:T(8,128)(2,1)S(1)}, bf16[3,3,128,128]{3,2,1,0:T(8,128)(2,1)}, u32[]{:S(2)}) copy-start(bf16[3,3,128,128]{3,2,1,0:T(8,128)(2,1)} %param.6) | copy-start | bytes 884740
  7.2 9.2 %copy-start.12 = (bf16[1,128,32,128]{3,2,1,0:T(8,128)(2,1)S(1)}, bf16[1,128,32,128]{3,2,1,0:T(8,128)(2,1)}, u32[]{:S(2)}) copy-start(bf16[1,128,32,128]{3,2,1,0:T(8,128)(2,1)} %param.7) | copy-start | bytes 3145732
  7.2 372.6 %all-reduce.5.cloned.1.call-start = ((), (), s32[]{:S(2)}) async-start(), calls=%async_computation | async-start | bytes 1998848 | tf_op jit(solution)/shard_map/psum | solution.py:85
  9.3 17.1 %collective-permute-start.1 = (bf16[1,32,32,2]{3,1,2,0:T(8,128)(2,1)S(1)}, bf16[1,32,32,2]{3,1,2,0:T(8,128)(2,1)S(1)}, u32[]{:S(2)}, u32[]{:S(2)}) collective-permute-start(bf16[1,32,32,2]{3,1,2,0:T(8,128)(2,1)S(1)} %get-tuple-element.20), channel_id=1, source_target_pairs={{16,0},{32,16},{48,32},{64,48},{80,64},{96,80},{112,96},{128,112},... | collective-permute-start | bytes 12296 | tf_op jit(solution)/shard_map/ppermute | solution.py:18
  10.6 15.8 %collective-permute-start = (bf16[1,32,32,2]{3,1,2,0:T(8,128)(2,1)S(1)}, bf16[1,32,32,2]{3,1,2,0:T(8,128)(2,1)S(1)}, u32[]{:S(2)}, u32[]{:S(2)}) collective-permute-start(bf16[1,32,32,2]{3,1,2,0:T(8,128)(2,1)S(1)} %get-tuple-element.19), channel_id=1, source_target_pairs={{0,16},{16,32},{32,48},{48,64},{64,80},{80,96},{96,112},{112,128},... | collective-permute-start | bytes 12296 | tf_op jit(solution)/shard_map/ppermute | solution.py:15
  26.4 0.7 copy-start.11
  28.5 3.0 copy-start.15
  28.7 2.8 copy-start.14
  42.6 11.2 %collective-permute-start.3 = (bf16[1,128,32,2]{1,2,3,0:T(8,128)(2,1)S(1)}, bf16[1,128,32,2]{1,2,3,0:T(8,128)(2,1)S(1)}, u32[]{:S(2)}, u32[]{:S(2)}) collective-permute-start(bf16[1,128,32,2]{1,2,3,0:T(8,128)(2,1)S(1)} %copy.62), channel_id=1, source_target_pairs={{16,0},{32,16},{48,32},{64,48},{80,64},{96,80},{112,96},{128,112},... | collective-permute-start | bytes 49160 | tf_op jit(solution)/shard_map/ppermute | solution.py:18
  44.3 10.1 %collective-permute-start.2 = (bf16[1,128,32,2]{1,2,3,0:T(8,128)(2,1)S(1)}, bf16[1,128,32,2]{1,2,3,0:T(8,128)(2,1)S(1)}, u32[]{:S(2)}, u32[]{:S(2)}) collective-permute-start(bf16[1,128,32,2]{1,2,3,0:T(8,128)(2,1)S(1)} %copy.61), channel_id=1, source_target_pairs={{0,16},{16,32},{32,48},{48,64},{64,80},{80,96},{96,112},{112,128},... | collective-permute-start | bytes 49160 | tf_op jit(solution)/shard_map/ppermute | solution.py:15
  54.4 5.3 %copy-start.2 = (bf16[1,128,32,2]{3,1,2,0:T(8,128)(2,1)}, bf16[1,128,32,2]{3,1,2,0:T(8,128)(2,1)S(1)}, u32[]{:S(2)}) copy-start(bf16[1,128,32,2]{3,1,2,0:T(8,128)(2,1)S(1)} %copy.64) | copy-start | bytes 49156
  55.8 3.9 copy-start.4
  71.0 1.2 copy-start.8
  72.5 1.0 copy-start.6
  75.4 2.3 copy-start.1
  79.9 1.2 copy-start.3
  81.2 1.3 copy-start.5
  82.4 10.5 %copy-start.7 = (bf16[1,128,32,128]{1,2,3,0:T(8,128)(2,1)S(1)}, bf16[1,128,32,128]{1,2,3,0:T(8,128)(2,1)}, u32[]{:S(2)}) copy-start(bf16[1,128,32,128]{1,2,3,0:T(8,128)(2,1)} %copy-done.6) | copy-start | bytes 3145732
  83.1 9.6 %collective-permute-start.5 = (bf16[1,128,32,2]{1,2,3,0:T(8,128)(2,1)}, bf16[1,128,32,2]{1,2,3,0:T(8,128)(2,1)S(1)}, u32[]{:S(2)}, u32[]{:S(2)}) collective-permute-start(bf16[1,128,32,2]{1,2,3,0:T(8,128)(2,1)} %get-tuple-element.14), channel_id=1, source_target_pairs={{16,0},{32,16},{48,32},{64,48},{80,64},{96,80},{112,96},{128,112},... | collective-permute-start | bytes 49160 | tf_op jit(solution)/shard_map/ppermute | solution.py:18
  84.4 8.6 %collective-permute-start.4 = (bf16[1,128,32,2]{1,2,3,0:T(8,128)(2,1)S(1)}, bf16[1,128,32,2]{1,2,3,0:T(8,128)(2,1)S(1)}, u32[]{:S(2)}, u32[]{:S(2)}) collective-permute-start(bf16[1,128,32,2]{1,2,3,0:T(8,128)(2,1)S(1)} %get-tuple-element.13), channel_id=1, source_target_pairs={{0,16},{16,32},{32,48},{48,64},{64,80},{80,96},{96,112},{112,128},... | collective-permute-start | bytes 49160 | tf_op jit(solution)/shard_map/ppermute | solution.py:15
  93.1 0.7 copy-start.16
  93.1 1.6 copy-start.17
  105.7 1.5 copy-start.13
  106.2 1.5 copy-start.9
  111.7 3.6 copy-start.10
Sparse Core Ops, SparseCore 0:
  115.4 264.3 all-reduce.4
where the time goes:
time: 391 us; the launch traced here: 390 us
  waiting for transfers between devices  270 us (69%)
  local copies, waits for them, and re-layouts  38.4 us (10%)
  matrix products  34.4 us (9%)
  starting transfers between devices  24.9 us (6%)
  between operations  14.7 us (4%)
  other arithmetic  8.07 us (2%)
    psum x1, waiting for transfers between devices, on_device(): grad_one, grad_two = lax.psum((local_one, local_two), ('track', 'rep'))  262 us
    unnamed x49, local copies, waits for them, and re-layouts  22.4 us
    ppermute x3, starting transfers between devices, extended(): lax.ppermute(lax.slice_in_dim(block, block.shape[dim] - width, None, axis...  21 us
    dot_general x34, matrix products, kernel_grad(): jnp.einsum('nchw,nfhw->cf', window, delta, preferred_element_type=jnp.flo...  18.6 us
    conv_general_dilated x3, matrix products, convolve(): lax.conv_general_dilated(lhs, kernel, (1, 1), ((2, 2), (0, 0)), rhs_dilat...  15.8 us
  transfers between devices with their start and end apart: 7, of which 3 were waited for; matrix products, arithmetic and copies ran while one was open for 2% of the time, Pallas kernels for 0%

commit v1 on v0

--- a/solution.py
+++ b/solution.py
@@ -82,7 +82,7 @@
     back_hidden = convolve(d_cols, flipped, 2)
     delta_one = (back_hidden * gelu_slope(pre_one)).astype(jnp.bfloat16)
     local_one = kernel_grad(pad_rows(x_cols), delta_one, 5, 1)
-    grad_one, grad_two = lax.psum((local_one, local_two), ("track", "rep"))
+    grad_one, grad_two = lax.psum(lax.psum((local_one, local_two), "rep"), "track")
     return (feature_map, grad_one, grad_two)
 
 

time: 391 us -> 432 us (1.10)
  waiting for transfers between devices: 270 us -> 311 us
    psum x1 -> x2, waiting for transfers between devices: 262 us -> 303 us  [the longest x1 176 us: on_device(): lax.psum(lax.psum((local_one, local_two), 'rep'), 'track')]
  transfers between devices with their start and end apart: 7 -> 8, of which waited for: 3 -> 4; matrix products, arithmetic and copies ran while one was open for 2% -> 2% of each run, Pallas kernels for 0% -> 0%
where the time goes in v1:
time: 432 us
  waiting for transfers between devices  311 us (72%)
  local copies, waits for them, and re-layouts  38.4 us (9%)
  matrix products  34.4 us (8%)
  starting transfers between devices  24.9 us (6%)
  between operations  14.7 us (3%)
  other arithmetic  8.07 us (2%)
    psum x1, waiting for transfers between devices, on_device(): lax.psum(lax.psum((local_one, local_two), 'rep'), 'track')  176 us
    psum x1, waiting for transfers between devices, on_device(): lax.psum((local_one, local_two), 'rep')  127 us
    unnamed x49, local copies, waits for them, and re-layouts  22.4 us
    ppermute x3, starting transfers between devices, extended(): lax.ppermute(lax.slice_in_dim(block, block.shape[dim] - width, None, axis...  20.9 us
    dot_general x34, matrix products, kernel_grad(): jnp.einsum('nchw,nfhw->cf', window, delta, preferred_element_type=jnp.flo...  18.6 us
    conv_general_dilated x3, matrix products, convolve(): lax.conv_general_dilated(lhs, kernel, (1, 1), ((2, 2), (0, 0)), rhs_dilat...  15.8 us
  transfers between devices with their start and end apart: 8, of which 4 were waited for; matrix products, arithmetic and copies ran while one was open for 2% of the time, Pallas kernels for 0%

profile of v1, /device:TPU:2, one launch (start us, length us, event | category | flops | bytes accessed | tf_op | source)
XLA Modules:
  0.0 431.6 jit_solution(17414880828660229014)
XLA Ops:
  7.2 1.9 constant_dynamic-update-slice_fusion.1
  9.3 1.3 collective-permute-start.1
  10.6 5.8 %collective-permute-start = (bf16[1,32,32,2]{3,1,2,0:T(8,128)(2,1)S(1)}, bf16[1,32,32,2]{3,1,2,0:T(8,128)(2,1)S(1)}, u32[]{:S(2)}, u32[]{:S(2)}) collective-permute-start(bf16[1,32,32,2]{3,1,2,0:T(8,128)(2,1)S(1)} %get-tuple-element.21), channel_id=1, source_target_pairs={{0,16},{16,32},{32,48},{48,64},{64,80},{80,96},{96,112},{112,128},... | collective-permute-start | bytes 12296 | tf_op jit(solution)/shard_map/ppermute | solution.py:15
  16.4 2.3 copy.69
  18.7 7.6 %collective-permute-done.1 = bf16[1,32,32,2]{3,1,2,0:T(8,128)(2,1)S(1)} collective-permute-done((bf16[1,32,32,2]{3,1,2,0:T(8,128)(2,1)S(1)}, bf16[1,32,32,2]{3,1,2,0:T(8,128)(2,1)S(1)}, u32[]{:S(2)}, u32[]{:S(2)}) %collective-permute-start.1) | collective-permute-done | bytes 4128 | tf_op jit(solution)/shard_map/ppermute | solution.py:18
  27.1 1.4 copy.92
  28.7 1.8 copy.58
  30.5 1.0 slice.177
  31.5 6.9 %multiply_convert_fusion.1 = (bf16[32,8,17,128]{3,1,2,0:T(8,128)(2,1)S(1)}, f32[32,8,17,128]{3,1,2,0:T(8,128)}) fusion(pred[8,17]{0,1:T(8,128)(4,1)S(1)} %copy-done.15, bf16[5,5,32,128]{3,2,1,0:T(8,128)(2,1)S(1)} %copy-done.14, bf16[32,32,1,7,4]{0,3,4,1,2:T(8,128)(2,1)S(1)} %slice.177, bf16[32,32,1,8,17]{0,3,4,1,2:T(8,128)(2,1)} %copy.58), kind=kOutput, calls=%fused_computation.22 | convolution fusion | flops 864468992 | bytes 3883144 | tf_op jit(solution)/shard_map/conv_general_dilated | solution.py:36
  38.6 1.0 copy.90
  39.6 1.4 fusion.196
  41.0 1.6 copy.62
  42.7 1.3 collective-permute-start.3
  44.3 7.8 %collective-permute-start.2 = (bf16[1,128,32,2]{1,2,3,0:T(8,128)(2,1)S(1)}, bf16[1,128,32,2]{1,2,3,0:T(8,128)(2,1)S(1)}, u32[]{:S(2)}, u32[]{:S(2)}) collective-permute-start(bf16[1,128,32,2]{1,2,3,0:T(8,128)(2,1)S(1)} %copy.61), channel_id=1, source_target_pairs={{0,16},{16,32},{32,48},{48,64},{64,80},{80,96},{96,112},{112,128},... | collective-permute-start | bytes 49160 | tf_op jit(solution)/shard_map/ppermute | solution.py:15
  52.1 1.7 constant_dynamic-update-slice_fusion
  54.4 1.4 copy.63
  55.8 3.9 fusion.230
  59.7 2.5 pad_maximum_fusion
  62.2 3.0 copy.93
  65.9 5.0 %fusion.12 = (f32[32,8,17,128]{3,1,2,0:T(8,128)S(1)}, bf16[32,8,17,128]{3,1,2,0:T(8,128)(2,1)}) fusion(pred[8,17]{0,1:T(8,128)(4,1)S(1)} %copy-done.15, bf16[3,3,128,128]{3,2,1,0:T(8,128)(2,1)S(1)} %copy-done, bf16[128,32,1,7,4]{0,3,4,1,2:T(8,128)(2,1)S(1)} %slice.181, bf16[128,32,1,8,17]{0,3,4,1,2:T(8,128)(2,1)S(1)} %copy.67), kind=kOutput, calls=%fused_computation.18 | convolution fusion | flops 1245249536 | bytes 4980872 | tf_op jit(solution)/shard_map/conv_general_dilated | solution.py:36
  73.5 1.9 copy.78
  75.4 2.3 convolution_bitcast_fusion
  83.1 1.3 collective-permute-start.5
  84.4 7.3 %collective-permute-start.4 = (bf16[1,128,32,2]{1,2,3,0:T(8,128)(2,1)S(1)}, bf16[1,128,32,2]{1,2,3,0:T(8,128)(2,1)S(1)}, u32[]{:S(2)}, u32[]{:S(2)}) collective-permute-start(bf16[1,128,32,2]{1,2,3,0:T(8,128)(2,1)S(1)} %get-tuple-element.15), channel_id=1, source_target_pairs={{0,16},{16,32},{32,48},{48,64},{64,80},{80,96},{96,112},{112,128},... | collective-permute-start | bytes 49160 | tf_op jit(solution)/shard_map/ppermute | solution.py:15
  93.8 0.9 copy-done.17
  94.7 3.9 fusion.7
  98.9 1.0 copy.91
  115.3 127.2 %all-reduce.7.cloned.1.call-done = (f32[5,5,32,128]{3,2,1,0:T(8,128)}, f32[3,3,128,128]{3,2,1,0:T(8,128)}) async-done(((f32[5,5,32,128]{3,2,1,0:T(8,128)}, f32[3,3,128,128]{3,2,1,0:T(8,128)}), (f32[5,5,32,128]{3,2,1,0:T(8,128)}, f32[3,3,128,128]{3,2,1,0:T(8,128)})) %all-reduce.7.cloned.1.call-update) | async-done | bytes 999440 | tf_op jit(solution)/shard_map/psum | solution.py:85
  242.7 2.3 copy.89
  245.0 176.1 %all-reduce.9.cloned.1.call-done = (f32[5,5,32,128]{3,2,1,0:T(8,128)}, f32[3,3,128,128]{3,2,1,0:T(8,128)}) async-done(((f32[5,5,32,128]{3,2,1,0:T(8,128)}, f32[3,3,128,128]{3,2,1,0:T(8,128)}), (f32[5,5,32,128]{3,2,1,0:T(8,128)}, f32[3,3,128,128]{3,2,1,0:T(8,128)})) %all-reduce.9.cloned.1.call-update) | async-done | bytes 999440 | tf_op jit(solution)/shard_map/psum | solution.py:85
  421.1 1.8 copy.127
  422.8 1.9 copy.128
  (106 shorter events, 28.5 us)
Async XLA Ops:
  7.2 58.7 %copy-start = (bf16[3,3,128,128]{3,2,1,0:T(8,128)(2,1)S(1)}, bf16[3,3,128,128]{3,2,1,0:T(8,128)(2,1)}, u32[]{:S(2)}) copy-start(bf16[3,3,128,128]{3,2,1,0:T(8,128)(2,1)} %param.6) | copy-start | bytes 884740
  7.2 9.2 %copy-start.12 = (bf16[1,128,32,128]{3,2,1,0:T(8,128)(2,1)S(1)}, bf16[1,128,32,128]{3,2,1,0:T(8,128)(2,1)}, u32[]{:S(2)}) copy-start(bf16[1,128,32,128]{3,2,1,0:T(8,128)(2,1)} %param.7) | copy-start | bytes 3145732
  7.2 235.2 %all-reduce.7.cloned.1.call-start = ((), (), s32[]{:S(2)}) async-start(), calls=%async_computation | async-start | bytes 1998848 | tf_op jit(solution)/shard_map/psum | solution.py:85
  9.3 17.1 %collective-permute-start.1 = (bf16[1,32,32,2]{3,1,2,0:T(8,128)(2,1)S(1)}, bf16[1,32,32,2]{3,1,2,0:T(8,128)(2,1)S(1)}, u32[]{:S(2)}, u32[]{:S(2)}) collective-permute-start(bf16[1,32,32,2]{3,1,2,0:T(8,128)(2,1)S(1)} %get-tuple-element.22), channel_id=1, source_target_pairs={{16,0},{32,16},{48,32},{64,48},{80,64},{96,80},{112,96},{128,112},... | collective-permute-start | bytes 12296 | tf_op jit(solution)/shard_map/ppermute | solution.py:18
  10.6 15.8 %collective-permute-start = (bf16[1,32,32,2]{3,1,2,0:T(8,128)(2,1)S(1)}, bf16[1,32,32,2]{3,1,2,0:T(8,128)(2,1)S(1)}, u32[]{:S(2)}, u32[]{:S(2)}) collective-permute-start(bf16[1,32,32,2]{3,1,2,0:T(8,128)(2,1)S(1)} %get-tuple-element.21), channel_id=1, source_target_pairs={{0,16},{16,32},{32,48},{48,64},{64,80},{80,96},{96,112},{112,128},... | collective-permute-start | bytes 12296 | tf_op jit(solution)/shard_map/ppermute | solution.py:15
  26.4 0.7 copy-start.11
  28.5 3.0 copy-start.15
  28.7 2.8 copy-start.14
  42.7 11.2 %collective-permute-start.3 = (bf16[1,128,32,2]{1,2,3,0:T(8,128)(2,1)S(1)}, bf16[1,128,32,2]{1,2,3,0:T(8,128)(2,1)S(1)}, u32[]{:S(2)}, u32[]{:S(2)}) collective-permute-start(bf16[1,128,32,2]{1,2,3,0:T(8,128)(2,1)S(1)} %copy.62), channel_id=1, source_target_pairs={{16,0},{32,16},{48,32},{64,48},{80,64},{96,80},{112,96},{128,112},... | collective-permute-start | bytes 49160 | tf_op jit(solution)/shard_map/ppermute | solution.py:18
  44.3 10.1 %collective-permute-start.2 = (bf16[1,128,32,2]{1,2,3,0:T(8,128)(2,1)S(1)}, bf16[1,128,32,2]{1,2,3,0:T(8,128)(2,1)S(1)}, u32[]{:S(2)}, u32[]{:S(2)}) collective-permute-start(bf16[1,128,32,2]{1,2,3,0:T(8,128)(2,1)S(1)} %copy.61), channel_id=1, source_target_pairs={{0,16},{16,32},{32,48},{48,64},{64,80},{80,96},{96,112},{112,128},... | collective-permute-start | bytes 49160 | tf_op jit(solution)/shard_map/ppermute | solution.py:15
  54.4 5.3 %copy-start.2 = (bf16[1,128,32,2]{3,1,2,0:T(8,128)(2,1)}, bf16[1,128,32,2]{3,1,2,0:T(8,128)(2,1)S(1)}, u32[]{:S(2)}) copy-start(bf16[1,128,32,2]{3,1,2,0:T(8,128)(2,1)S(1)} %copy.64) | copy-start | bytes 49156
  55.8 3.9 copy-start.4
  71.0 1.2 copy-start.8
  72.5 1.0 copy-start.6
  75.4 2.3 copy-start.1
  79.9 1.2 copy-start.3
  81.2 1.3 copy-start.5
  82.4 10.5 %copy-start.7 = (bf16[1,128,32,128]{1,2,3,0:T(8,128)(2,1)S(1)}, bf16[1,128,32,128]{1,2,3,0:T(8,128)(2,1)}, u32[]{:S(2)}) copy-start(bf16[1,128,32,128]{1,2,3,0:T(8,128)(2,1)} %copy-done.6) | copy-start | bytes 3145732
  83.1 9.6 %collective-permute-start.5 = (bf16[1,128,32,2]{1,2,3,0:T(8,128)(2,1)}, bf16[1,128,32,2]{1,2,3,0:T(8,128)(2,1)S(1)}, u32[]{:S(2)}, u32[]{:S(2)}) collective-permute-start(bf16[1,128,32,2]{1,2,3,0:T(8,128)(2,1)} %get-tuple-element.16), channel_id=1, source_target_pairs={{16,0},{32,16},{48,32},{64,48},{80,64},{96,80},{112,96},{128,112},... | collective-permute-start | bytes 49160 | tf_op jit(solution)/shard_map/ppermute | solution.py:18
  84.4 8.5 %collective-permute-start.4 = (bf16[1,128,32,2]{1,2,3,0:T(8,128)(2,1)S(1)}, bf16[1,128,32,2]{1,2,3,0:T(8,128)(2,1)S(1)}, u32[]{:S(2)}, u32[]{:S(2)}) collective-permute-start(bf16[1,128,32,2]{1,2,3,0:T(8,128)(2,1)S(1)} %get-tuple-element.15), channel_id=1, source_target_pairs={{0,16},{16,32},{32,48},{48,64},{64,80},{80,96},{96,112},{112,128},... | collective-permute-start | bytes 49160 | tf_op jit(solution)/shard_map/ppermute | solution.py:15
  93.1 0.7 copy-start.16
  93.1 1.6 copy-start.17
  105.7 1.5 copy-start.13
  106.2 1.5 copy-start.9
  112.1 130.3 %copy-start.10 = (bf16[32,8,17,128]{3,1,2,0:T(8,128)(2,1)S(1)}, bf16[32,8,17,128]{3,1,2,0:T(8,128)(2,1)}, u32[]{:S(2)}) copy-start(bf16[32,8,17,128]{3,1,2,0:T(8,128)(2,1)} %get-tuple-element.14) | copy-start | bytes 3342340
  115.2 305.8 %all-reduce.9.cloned.1.call-start = ((), (), s32[]{:S(2)}) async-start(), calls=%async_computation.1 | async-start | bytes 1998848 | tf_op jit(solution)/shard_map/psum | solution.py:85
Sparse Core Ops, SparseCore 0:
  115.4 127.0 all-reduce.6
  245.4 175.6 all-reduce.8
